TPU v7x, 32 devices: a whole 2x2x4 slice. The times are simulated.
32 devices in a mesh: comp: 2 (over core), tile: 8 (over z, y), lev: 2 (over x).
Axes of the slice: x: 2, y: 2, z: 4, core: 2. Of those that a mesh axis runs over, the one named last changes fastest.
Arguments:
- climate_departure: bfloat16 [128, 64, 1024], P(('comp', 'lev'), None, 'tile'), may hold values from -6 to 6
- spread_rate: float32 [64, 1024], P(None, 'tile'), may hold values from 0.02 to 0.15
- advection_fraction: float32 [128], P(('comp', 'lev')), may hold values from 0.05 to 0.3
- blend_kernel_excess: bfloat16 [128, 128], P(('comp', 'lev')), may hold values from -0.5 to 0.5
- layer_emission_share: bfloat16 [4, 128], replicated, may hold values from -0.5 to 0.5
- link_coupling_submatrix: bfloat16 [8, 16, 128, 128], P('tile'), may hold values from -0.5 to 0.5
- link_provider_group: int32 [8, 16], P('tile'), may hold values from 0 to 7, as said below
- occupied_link_total: int32 [8], P('tile'), may hold values from 4 to 16, as said below
- water_top_departure: float32 [64, 1024], P(None, 'tile'), may hold values from -6 to 6
- pond_spread_rate: float32 [64, 1024], P(None, 'tile'), may hold values from 0.02 to 0.2
- water_reaction: float32 [4], replicated, may hold values from 0.1 to 0.5
Outputs:
- stepped_climate: bfloat16 [128, 64, 1024], P(('comp', 'lev'), None, 'tile')
- water_top_later: float32 [64, 1024], P(None, 'tile')
Inputs may be any that keep to these rules, and one draw needn't show every extreme that they name: `link_provider_group`: slots b >= occupied_link_total[t] of ocean tile t are unused. Slot 0 of ocean tile t names atmosphere tile t. Every slot of ocean tile t names a tile at most 3 tiles away from t along the periodic circle of tiles. `occupied_link_total`: some ocean tile uses all 16 slots.
All inputs are finite; a program needn't handle non-finite values.
Results may differ from a plain program's by a relative error of at most 0.0051.
Values may be sent and summed in bfloat16 or wider, within the bound.
A program may use at most 64 MiB of HBM per device.

v0:
```python
import jax
import jax.numpy as jnp
from jax import lax
from jax.sharding import PartitionSpec as P

REACH_MOST = 8


def with_halo(value, sides, width):
    for axis, dim in sides:
        devices, length = (lax.axis_size(axis), value.shape[dim])
        up = [(i, (i + 1) % devices) for i in range(devices)]
        down = [(j, i) for i, j in up]
        last = lax.slice_in_dim(value, length - width, length, axis=dim)
        first = lax.slice_in_dim(value, 0, width, axis=dim)
        before = lax.ppermute(last, axis, up)
        after = lax.ppermute(first, axis, down)
        value = jnp.concatenate([before, value, after], axis=dim)
    return value


def passed_along(block, axis, distance):
    devices = range(lax.axis_size(axis))
    route = [((i - distance) % len(devices), i) for i in devices]
    return lax.ppermute(block, axis, route)


def on_device(
    climate_departure,
    spread_rate,
    advection_fraction,
    blend_kernel_excess,
    layer_emission_share,
    link_coupling_submatrix,
    link_provider_group,
    occupied_link_total,
    water_top_departure,
    pond_spread_rate,
    water_reaction,
):
    depth, rows, width = climate_departure.shape
    fields = layer_emission_share.shape[0]
    most = link_coupling_submatrix.shape[1]
    extended = with_halo(climate_departure, (("tile", 2),), 1)
    field = climate_departure.astype(jnp.float32)
    west = extended[:, :, :-2].astype(jnp.float32)
    east = extended[:, :, 2:].astype(jnp.float32)
    padded = jnp.pad(field, ((0, 0), (1, 1), (0, 0)))
    lap = padded[:, 2:, :] + padded[:, :-2, :] + east + west - 4.0 * field
    advected = (
        field + spread_rate[None] * lap - advection_fraction[:, None, None] * (field - west)
    ).astype(jnp.bfloat16)
    piece = lax.all_gather(advected, ("comp", "lev"), axis=0, tiled=True)
    count = piece.shape[0]
    mix_total = jnp.dot(
        blend_kernel_excess, piece.reshape(count, -1), preferred_element_type=jnp.float32
    )
    subset = piece
    flux_total = jnp.dot(
        layer_emission_share, subset.reshape(count, -1), preferred_element_type=jnp.float32
    )
    mix_total, flux_total = (mix_total, flux_total)
    stepped_climate = (advected.astype(jnp.float32) + mix_total.reshape(depth, rows, width)).astype(
        jnp.bfloat16
    )
    flux = flux_total.astype(jnp.bfloat16).reshape(1, fields * rows, width)
    sources = link_provider_group[0]
    live = jnp.arange(most) < occupied_link_total[0]
    tile_count = lax.axis_size("tile")
    tile_here = lax.axis_index("tile")
    reach = min(REACH_MOST, (tile_count - 1) // 2)

    def take_from(piece, anchor):
        picker = ((sources == anchor) & live).astype(jnp.bfloat16)
        return jnp.dot(picker[:, None], piece.reshape(1, -1), preferred_element_type=jnp.float32)

    picked = take_from(flux, tile_here)
    for offset in range(-reach, reach + 1):
        if offset != 0:
            nearby = passed_along(flux, "tile", offset)
            picked = picked + take_from(nearby, (tile_here - offset) % tile_count)
    blocks = picked.astype(jnp.bfloat16).reshape(most, fields * rows, width)
    ocean_flux = jnp.einsum(
        "bxc,bco->xo", blocks, link_coupling_submatrix[0], preferred_element_type=jnp.float32
    )
    ocean_flux = ocean_flux.reshape(fields, rows, -1)
    pond_enlarged_array = with_halo(
        water_top_departure.astype(jnp.bfloat16), (("tile", 1),), 1
    ).astype(water_top_departure.dtype)
    pond_halo_array = jnp.pad(water_top_departure, ((1, 1), (0, 0)))
    pond_second_derivative_sum = (
        pond_halo_array[2:]
        + pond_halo_array[:-2]
        + pond_enlarged_array[:, :-2]
        + pond_enlarged_array[:, 2:]
        - 4.0 * water_top_departure
    )
    bottom_layer_push = jnp.sum(water_reaction[:, None, None] * ocean_flux, axis=0)
    water_top_later = (
        water_top_departure + pond_spread_rate * pond_second_derivative_sum + bottom_layer_push
    )
    return (stepped_climate, water_top_later)


def solution(mesh):
    in_specs = (
        P(("comp", "lev"), None, "tile"),
        P(None, "tile"),
        P(("comp", "lev")),
        P(("comp", "lev"), None),
        P(),
        P("tile", None, None, None),
        P("tile", None),
        P("tile"),
        P(None, "tile"),
        P(None, "tile"),
        P(),
    )
    out_specs = (P(("comp", "lev"), None, "tile"), P(None, "tile"))
    return jax.shard_map(
        on_device, mesh=mesh, in_specs=in_specs, out_specs=out_specs, check_vma=False
    )
```

profile of v0, /device:TPU:0, one launch (start us, length us, event | category | flops | bytes accessed | tf_op | source)
XLA Modules:
  0.0 90.8 jit_solution(7648104784000251665)
XLA Ops:
  7.2 0.0 copy-start
  7.2 0.0 copy-start.1
  7.2 0.0 copy-start.10
  7.2 0.0 copy-start.5
  7.2 0.0 all-gather.2.cloned.1.call-start
  7.3 1.5 %fusion.36 = (bf16[32,64,1]{2,1,0:T(8,128)(2,1)S(1)}, bf16[32,64,1]{2,1,0:T(8,128)(2,1)S(1)}) fusion(bf16[32,64,128]{2,1,0:T(8,128)(2,1)} %param.11), kind=kLoop, calls=%fused_computation.62 | loop fusion | bytes 16384 | tf_op jit(solution)/shard_map/slice | solution.py:15
  8.8 6.1 %collective-permute-start = (bf16[32,64,1]{2,1,0:T(8,128)(2,1)S(1)}, bf16[32,64,1]{2,1,0:T(8,128)(2,1)S(1)}, u32[]{:S(2)}, u32[]{:S(2)}) collective-permute-start(bf16[32,64,1]{2,1,0:T(8,128)(2,1)S(1)} %get-tuple-element.2), channel_id=1, source_target_pairs={{2,0},{4,2},{6,4},{8,6},{10,8},{12,10},{14,12},{0,14},{3,1},{5,3},... | collective-permute-start | bytes 12296 | tf_op jit(solution)/shard_map/ppermute | solution.py:17
  14.8 0.0 collective-permute-start.1
  14.8 0.0 copy-done.1
  14.8 0.1 convert_element_type.44
  15.0 0.0 copy-start.4
  15.0 0.0 copy-start.9
  15.0 0.0 copy-start.11
  15.0 20.0 %collective-permute-done = bf16[32,64,1]{2,1,0:T(8,128)(2,1)S(1)} collective-permute-done((bf16[32,64,1]{2,1,0:T(8,128)(2,1)S(1)}, bf16[32,64,1]{2,1,0:T(8,128)(2,1)S(1)}, u32[]{:S(2)}, u32[]{:S(2)}) %collective-permute-start) | collective-permute-done | bytes 4128 | tf_op jit(solution)/shard_map/ppermute | solution.py:17
  35.0 0.2 collective-permute-done.1
  35.1 0.0 copy-done.10
  35.1 0.0 copy-done.5
  35.1 1.9 %fusion.18 = bf16[32,64,128]{2,1,0:T(8,128)(2,1)} fusion(f32[32,64,128]{2,1,0:T(8,128)S(1)} %convert_element_type.44, bf16[32,64,128]{2,1,0:T(8,128)(2,1)S(1)} %copy-done.1, bf16[32,64,1]{2,1,0:T(8,128)(2,1)S(1)} %collective-permute-done.1, bf16[32,64,1]{2,1,0:T(8,128)(2,1)S(1)} %collective-permute-done, f32[32]{0:T(128)S(1)} %copy-done.10, ...), kind=kLoop, calls=%fused_computation.23 | loop fusion | flops 4980736 | bytes 2138240 | tf_op jit(solution)/shard_map/convert_element_type | solution.py:52
  37.0 0.0 copy-start.7
  37.0 0.0 all-gather.2.cloned.1.call-update
  37.1 0.0 copy-done.4
  37.1 0.1 fusion.37
  37.2 2.5 %collective-permute-start.2 = (bf16[64,1]{1,0:T(8,128)(2,1)S(1)}, bf16[64,1]{1,0:T(8,128)(2,1)S(1)}, u32[]{:S(2)}, u32[]{:S(2)}) collective-permute-start(bf16[64,1]{1,0:T(8,128)(2,1)S(1)} %get-tuple-element.4), channel_id=1, source_target_pairs={{0,2},{2,4},{4,6},{6,8},{8,10},{10,12},{12,14},{14,0},{1,3},{3,5},... | collective-permute-start | bytes 392 | tf_op jit(solution)/shard_map/ppermute | solution.py:16
  39.6 2.4 %collective-permute-start.3 = (bf16[64,1]{1,0:T(8,128)(2,1)S(1)}, bf16[64,1]{1,0:T(8,128)(2,1)S(1)}, u32[]{:S(2)}, u32[]{:S(2)}) collective-permute-start(bf16[64,1]{1,0:T(8,128)(2,1)S(1)} %get-tuple-element.5), channel_id=1, source_target_pairs={{2,0},{4,2},{6,4},{8,6},{10,8},{12,10},{14,12},{0,14},{3,1},{5,3},... | collective-permute-start | bytes 392 | tf_op jit(solution)/shard_map/ppermute | solution.py:17
  42.8 0.0 copy-done.9
  42.8 0.9 %collective-permute-done.2 = bf16[64,1]{1,0:T(8,128)(2,1)S(1)} collective-permute-done((bf16[64,1]{1,0:T(8,128)(2,1)S(1)}, bf16[64,1]{1,0:T(8,128)(2,1)S(1)}, u32[]{:S(2)}, u32[]{:S(2)}) %collective-permute-start.2) | collective-permute-done | bytes 160 | tf_op jit(solution)/shard_map/ppermute | solution.py:16
  43.7 0.0 collective-permute-done.3
  43.7 0.1 maximum_convert_fusion
  43.8 17.5 %all-gather.2.cloned.1.call-done = bf16[128,64,128]{2,1,0:T(8,128)(2,1)} async-done(((bf16[32,64,128]{2,1,0:T(8,128)(2,1)}), bf16[128,64,128]{2,1,0:T(8,128)(2,1)}) %all-gather.2.cloned.1.call-update) | async-done | bytes 2097168 | tf_op jit(solution)/shard_map/all_gather | solution.py:53
  61.3 0.0 copy-start.3
  61.3 0.0 copy-done.11
  61.4 3.0 %fusion = bf16[4,8192]{1,0:T(4,128)(2,1)S(1)} fusion(bf16[4,128]{1,0:T(4,128)(2,1)S(1)} %copy-done.11, bf16[16,8,64,128]{3,2,1,0:T(8,128)(2,1)} %bitcast.80), kind=kOutput, calls=%fused_computation.1 | convolution fusion | flops 8421376 | bytes 2163712 | tf_op jit(solution)/shard_map/dot_general | solution.py:59
  64.3 0.1 reshape.151
  64.4 0.0 copy-start.2
  64.4 2.4 %collective-permute-start.9 = (bf16[1,256,128]{2,1,0:T(8,128)(2,1)S(1)}, bf16[1,256,128]{2,1,0:T(8,128)(2,1)S(1)}, u32[]{:S(2)}, u32[]{:S(2)}) collective-permute-start(bf16[1,256,128]{2,1,0:T(8,128)(2,1)S(1)} %reshape.151), channel_id=1, source_target_pairs={{10,0},{12,2},{14,4},{0,6},{2,8},{4,10},{6,12},{8,14},{11,1},{13,3... | collective-permute-start | bytes 196616 | tf_op jit(solution)/shard_map/ppermute | solution.py:25
  66.9 1.5 %collective-permute-start.8 = (bf16[1,256,128]{2,1,0:T(8,128)(2,1)S(1)}, bf16[1,256,128]{2,1,0:T(8,128)(2,1)S(1)}, u32[]{:S(2)}, u32[]{:S(2)}) collective-permute-start(bf16[1,256,128]{2,1,0:T(8,128)(2,1)S(1)} %reshape.151), channel_id=1, source_target_pairs={{12,0},{14,2},{0,4},{2,6},{4,8},{6,10},{8,12},{10,14},{13,1},{15,3... | collective-permute-start | bytes 196616 | tf_op jit(solution)/shard_map/ppermute | solution.py:25
  68.3 1.5 %collective-permute-start.7 = (bf16[1,256,128]{2,1,0:T(8,128)(2,1)S(1)}, bf16[1,256,128]{2,1,0:T(8,128)(2,1)S(1)}, u32[]{:S(2)}, u32[]{:S(2)}) collective-permute-start(bf16[1,256,128]{2,1,0:T(8,128)(2,1)S(1)} %reshape.151), channel_id=1, source_target_pairs={{14,0},{0,2},{2,4},{4,6},{6,8},{8,10},{10,12},{12,14},{15,1},{1,3}... | collective-permute-start | bytes 196616 | tf_op jit(solution)/shard_map/ppermute | solution.py:25
  69.8 3.2 %collective-permute-start.6 = (bf16[1,256,128]{2,1,0:T(8,128)(2,1)S(1)}, bf16[1,256,128]{2,1,0:T(8,128)(2,1)S(1)}, u32[]{:S(2)}, u32[]{:S(2)}) collective-permute-start(bf16[1,256,128]{2,1,0:T(8,128)(2,1)S(1)} %reshape.151), channel_id=1, source_target_pairs={{2,0},{4,2},{6,4},{8,6},{10,8},{12,10},{14,12},{0,14},{3,1},{5,3},... | collective-permute-start | bytes 196616 | tf_op jit(solution)/shard_map/ppermute | solution.py:25
  73.1 0.5 collective-permute-start.5
  73.6 0.0 copy-done.7
  73.6 0.0 copy-done.3
  73.6 1.4 %fusion.6 = f32[4,8,64,128]{3,1,2,0:T(8,128)S(1)} fusion(bf16[32,128]{1,0:T(8,128)(2,1)S(1)} %copy-done.7, bf16[16,8,64,128]{3,2,1,0:T(8,128)(2,1)S(1)} %bitcast.81), kind=kOutput, calls=%fused_computation.8 | convolution fusion | flops 67108864 | bytes 3153920 | tf_op jit(solution)/shard_map/dot_general | solution.py:55
  75.0 0.2 copy.22
  75.2 0.0 copy-done.2
  75.2 1.0 %fusion.20 = bf16[32,64,128]{2,1,0:T(8,128)(2,1)} fusion(f32[4,8,64,128]{3,2,1,0:T(8,128)S(1)} %copy.22, bf16[32,64,128]{2,1,0:T(8,128)(2,1)S(1)} %copy-done.2), kind=kLoop, calls=%fused_computation.26 | loop fusion | flops 786432 | bytes 2097152 | tf_op jit(solution)/shard_map/convert_element_type | solution.py:63
  76.2 0.0 collective-permute-done.9
  76.2 0.1 collective-permute-start.4
  76.3 0.0 collective-permute-done.8
  76.3 0.0 collective-permute-done.7
  76.3 0.0 collective-permute-done.6
  76.4 1.0 %collective-permute-done.5 = bf16[1,256,128]{2,1,0:T(8,128)(2,1)S(1)} collective-permute-done((bf16[1,256,128]{2,1,0:T(8,128)(2,1)S(1)}, bf16[1,256,128]{2,1,0:T(8,128)(2,1)S(1)}, u32[]{:S(2)}, u32[]{:S(2)}) %collective-permute-start.5) | collective-permute-done | bytes 65568 | tf_op jit(solution)/shard_map/ppermute | solution.py:25
  77.4 0.0 copy-start.8
  77.4 4.0 %collective-permute-done.4 = bf16[1,256,128]{2,1,0:T(8,128)(2,1)S(1)} collective-permute-done((bf16[1,256,128]{2,1,0:T(8,128)(2,1)S(1)}, bf16[1,256,128]{2,1,0:T(8,128)(2,1)S(1)}, u32[]{:S(2)}, u32[]{:S(2)}) %collective-permute-start.4) | collective-permute-done | bytes 65568 | tf_op jit(solution)/shard_map/ppermute | solution.py:25
  81.4 1.0 %fusion.11 = bf16[2,8,256,128]{3,1,2,0:T(8,128)(2,1)S(1)} fusion(f32[32768]{0:T(1024)S(1)} %bitcast_convert_fusion, f32[16]{0:T(128)S(1)} %get-tuple-element.11, f32[32768]{0:T(1024)S(1)} %bitcast_convert_fusion.1, f32[16]{0:T(128)S(1)} %get-tuple-element.12, f32[32768]{0:T(1024)S(1)} %bitcast_convert_fusion.2, f32[16]{0:T(128)S(1)} %get-tuple-element.7, ...), kind=kLoop, calls=%fused_computation.16 | loop fusion | flops 7340032 | bytes 1966528
  82.4 0.0 copy-start.6
  82.5 0.2 copy.24
  82.7 0.0 copy-done
  82.7 0.0 copy-done.8
  82.7 0.4 fusion.10
  83.1 0.1 copy-done.6
  83.2 0.7 fusion.28
  (10 shorter events, 0.1 us)
Async XLA Ops:
  7.2 75.5 %copy-start = (bf16[1,16,128,128]{3,2,1,0:T(8,128)(2,1)S(1)}, bf16[1,16,128,128]{3,2,1,0:T(8,128)(2,1)}, u32[]{:S(2)}) copy-start(bf16[1,16,128,128]{3,2,1,0:T(8,128)(2,1)} %param.16) | copy-start | bytes 1572868
  7.2 7.7 %copy-start.1 = (bf16[32,64,128]{2,1,0:T(8,128)(2,1)S(1)}, bf16[32,64,128]{2,1,0:T(8,128)(2,1)}, u32[]{:S(2)}) copy-start(bf16[32,64,128]{2,1,0:T(8,128)(2,1)} %param.11) | copy-start | bytes 1572868
  7.2 27.9 %copy-start.10 = (f32[32]{0:T(128)S(1)}, f32[32]{0:T(128)}, u32[]{:S(2)}) copy-start(f32[32]{0:T(128)} %param.13) | copy-start | bytes 388
  7.2 27.9 %copy-start.5 = (f32[64,128]{1,0:T(8,128)S(1)}, f32[64,128]{1,0:T(8,128)}, u32[]{:S(2)}) copy-start(f32[64,128]{1,0:T(8,128)} %param.12) | copy-start | bytes 98308
  7.2 54.1 %all-gather.2.cloned.1.call-start = ((), (), s32[]{:S(2)}) async-start(), calls=%async_computation | async-start | bytes 2621440 | tf_op jit(solution)/shard_map/all_gather | solution.py:53
  8.8 26.2 %collective-permute-start = (bf16[32,64,1]{2,1,0:T(8,128)(2,1)S(1)}, bf16[32,64,1]{2,1,0:T(8,128)(2,1)S(1)}, u32[]{:S(2)}, u32[]{:S(2)}) collective-permute-start(bf16[32,64,1]{2,1,0:T(8,128)(2,1)S(1)} %get-tuple-element.2), channel_id=1, source_target_pairs={{2,0},{4,2},{6,4},{8,6},{10,8},{12,10},{14,12},{0,14},{3,1},{5,3},... | collective-permute-start | bytes 12296 | tf_op jit(solution)/shard_map/ppermute | solution.py:17
  14.8 20.3 %collective-permute-start.1 = (bf16[32,64,1]{2,1,0:T(8,128)(2,1)S(1)}, bf16[32,64,1]{2,1,0:T(8,128)(2,1)S(1)}, u32[]{:S(2)}, u32[]{:S(2)}) collective-permute-start(bf16[32,64,1]{2,1,0:T(8,128)(2,1)S(1)} %get-tuple-element.3), channel_id=1, source_target_pairs={{0,2},{2,4},{4,6},{6,8},{8,10},{10,12},{12,14},{14,0},{1,3},{3,5},... | collective-permute-start | bytes 12296 | tf_op jit(solution)/shard_map/ppermute | solution.py:16
  15.0 22.1 %copy-start.4 = (f32[64,128]{1,0:T(8,128)S(1)}, f32[64,128]{1,0:T(8,128)}, u32[]{:S(2)}) copy-start(f32[64,128]{1,0:T(8,128)} %param.19) | copy-start | bytes 98308
  15.0 27.8 %copy-start.9 = (s32[1,16]{1,0:T(1,128)S(1)}, s32[1,16]{1,0:T(1,128)}, u32[]{:S(2)}) copy-start(s32[1,16]{1,0:T(1,128)} %param.17) | copy-start | bytes 196
  15.0 46.4 %copy-start.11 = (bf16[4,128]{1,0:T(4,128)(2,1)S(1)}, bf16[4,128]{1,0:T(4,128)(2,1)}, u32[]{:S(2)}) copy-start(bf16[4,128]{1,0:T(4,128)(2,1)} %param.15) | copy-start | bytes 3076
  37.0 36.6 %copy-start.7 = (bf16[32,128]{1,0:T(8,128)(2,1)S(1)}, bf16[32,128]{1,0:T(8,128)(2,1)}, u32[]{:S(2)}) copy-start(bf16[32,128]{1,0:T(8,128)(2,1)} %param.14) | copy-start | bytes 24580
  37.2 6.6 %collective-permute-start.2 = (bf16[64,1]{1,0:T(8,128)(2,1)S(1)}, bf16[64,1]{1,0:T(8,128)(2,1)S(1)}, u32[]{:S(2)}, u32[]{:S(2)}) collective-permute-start(bf16[64,1]{1,0:T(8,128)(2,1)S(1)} %get-tuple-element.4), channel_id=1, source_target_pairs={{0,2},{2,4},{4,6},{6,8},{8,10},{10,12},{12,14},{14,0},{1,3},{3,5},... | collective-permute-start | bytes 392 | tf_op jit(solution)/shard_map/ppermute | solution.py:16
  39.6 4.1 %collective-permute-start.3 = (bf16[64,1]{1,0:T(8,128)(2,1)S(1)}, bf16[64,1]{1,0:T(8,128)(2,1)S(1)}, u32[]{:S(2)}, u32[]{:S(2)}) collective-permute-start(bf16[64,1]{1,0:T(8,128)(2,1)S(1)} %get-tuple-element.5), channel_id=1, source_target_pairs={{2,0},{4,2},{6,4},{8,6},{10,8},{12,10},{14,12},{0,14},{3,1},{5,3},... | collective-permute-start | bytes 392 | tf_op jit(solution)/shard_map/ppermute | solution.py:17
  61.3 12.3 %copy-start.3 = (bf16[128,64,128]{2,1,0:T(8,128)(2,1)S(1)}, bf16[128,64,128]{2,1,0:T(8,128)(2,1)}, u32[]{:S(2)}) copy-start(bf16[128,64,128]{2,1,0:T(8,128)(2,1)} %all-gather.2.cloned.1.call-done) | copy-start | bytes 6291460
  64.4 10.8 %copy-start.2 = (bf16[32,64,128]{2,1,0:T(8,128)(2,1)S(1)}, bf16[32,64,128]{2,1,0:T(8,128)(2,1)}, u32[]{:S(2)}) copy-start(bf16[32,64,128]{2,1,0:T(8,128)(2,1)} %fusion.18) | copy-start | bytes 1572868
  64.4 11.8 %collective-permute-start.9 = (bf16[1,256,128]{2,1,0:T(8,128)(2,1)S(1)}, bf16[1,256,128]{2,1,0:T(8,128)(2,1)S(1)}, u32[]{:S(2)}, u32[]{:S(2)}) collective-permute-start(bf16[1,256,128]{2,1,0:T(8,128)(2,1)S(1)} %reshape.151), channel_id=1, source_target_pairs={{10,0},{12,2},{14,4},{0,6},{2,8},{4,10},{6,12},{8,14},{11,1},{13,3... | collective-permute-start | bytes 196616 | tf_op jit(solution)/shard_map/ppermute | solution.py:25
  66.9 9.4 %collective-permute-start.8 = (bf16[1,256,128]{2,1,0:T(8,128)(2,1)S(1)}, bf16[1,256,128]{2,1,0:T(8,128)(2,1)S(1)}, u32[]{:S(2)}, u32[]{:S(2)}) collective-permute-start(bf16[1,256,128]{2,1,0:T(8,128)(2,1)S(1)} %reshape.151), channel_id=1, source_target_pairs={{12,0},{14,2},{0,4},{2,6},{4,8},{6,10},{8,12},{10,14},{13,1},{15,3... | collective-permute-start | bytes 196616 | tf_op jit(solution)/shard_map/ppermute | solution.py:25
  68.3 8.0 %collective-permute-start.7 = (bf16[1,256,128]{2,1,0:T(8,128)(2,1)S(1)}, bf16[1,256,128]{2,1,0:T(8,128)(2,1)S(1)}, u32[]{:S(2)}, u32[]{:S(2)}) collective-permute-start(bf16[1,256,128]{2,1,0:T(8,128)(2,1)S(1)} %reshape.151), channel_id=1, source_target_pairs={{14,0},{0,2},{2,4},{4,6},{6,8},{8,10},{10,12},{12,14},{15,1},{1,3}... | collective-permute-start | bytes 196616 | tf_op jit(solution)/shard_map/ppermute | solution.py:25
  69.8 6.5 %collective-permute-start.6 = (bf16[1,256,128]{2,1,0:T(8,128)(2,1)S(1)}, bf16[1,256,128]{2,1,0:T(8,128)(2,1)S(1)}, u32[]{:S(2)}, u32[]{:S(2)}) collective-permute-start(bf16[1,256,128]{2,1,0:T(8,128)(2,1)S(1)} %reshape.151), channel_id=1, source_target_pairs={{2,0},{4,2},{6,4},{8,6},{10,8},{12,10},{14,12},{0,14},{3,1},{5,3},... | collective-permute-start | bytes 196616 | tf_op jit(solution)/shard_map/ppermute | solution.py:25
  73.1 4.3 %collective-permute-start.5 = (bf16[1,256,128]{2,1,0:T(8,128)(2,1)S(1)}, bf16[1,256,128]{2,1,0:T(8,128)(2,1)S(1)}, u32[]{:S(2)}, u32[]{:S(2)}) collective-permute-start(bf16[1,256,128]{2,1,0:T(8,128)(2,1)S(1)} %reshape.151), channel_id=1, source_target_pairs={{4,0},{6,2},{8,4},{10,6},{12,8},{14,10},{0,12},{2,14},{5,1},{7,3},... | collective-permute-start | bytes 196616 | tf_op jit(solution)/shard_map/ppermute | solution.py:25
  76.2 5.2 %collective-permute-start.4 = (bf16[1,256,128]{2,1,0:T(8,128)(2,1)S(1)}, bf16[1,256,128]{2,1,0:T(8,128)(2,1)S(1)}, u32[]{:S(2)}, u32[]{:S(2)}) collective-permute-start(bf16[1,256,128]{2,1,0:T(8,128)(2,1)S(1)} %reshape.151), channel_id=1, source_target_pairs={{6,0},{8,2},{10,4},{12,6},{14,8},{0,10},{2,12},{4,14},{7,1},{9,3},... | collective-permute-start | bytes 196616 | tf_op jit(solution)/shard_map/ppermute | solution.py:25
  77.4 5.3 %copy-start.8 = (f32[4]{0:T(128)S(1)}, f32[4]{0:T(128)}, u32[]{:S(2)}) copy-start(f32[4]{0:T(128)} %param.21) | copy-start | bytes 52
  82.4 0.8 copy-start.6
Sparse Core Ops, SparseCore 0:
  37.2 24.1 all-gather.1
where the time goes:
time: 91 us; the launch traced here: 90.8 us
  waiting for transfers between devices  43.6 us (48%)
  starting transfers between devices  20.3 us (22%)
  between operations  15 us (16%)
  other arithmetic  4.87 us (5%)
  matrix products  4.74 us (5%)
  local copies, waits for them, and re-layouts  2.24 us (2%)
    ppermute x2, waiting for transfers between devices, with_halo(): after = lax.ppermute(first, axis, down)  20 us
    all_gather x1, waiting for transfers between devices, on_device(): piece = lax.all_gather(advected, ('comp', 'lev'), axis=0, tiled=True)  17.5 us
    ppermute x6, starting transfers between devices, passed_along(): return lax.ppermute(block, axis, route)  9.26 us
    ppermute x2, starting transfers between devices, with_halo(): after = lax.ppermute(first, axis, down)  8.48 us
    ppermute x6, waiting for transfers between devices, passed_along(): return lax.ppermute(block, axis, route)  5.03 us
    dot_general x1, matrix products, on_device(): jnp.dot(layer_emission_share, subset.reshape(count, -1), preferred_elemen...  2.95 us
    ppermute x2, starting transfers between devices, with_halo(): before = lax.ppermute(last, axis, up)  2.48 us
    convert_element_type x1, other arithmetic, on_device(): advected = (field + spread_rate[None] * lap - advection_fraction[:, None,...  1.92 us
  transfers between devices with their start and end apart: 11, of which 6 were waited for; matrix products, arithmetic and copies ran while one was open for 3% of the time, Pallas kernels for 0%

commit v1 on v0

v1 whole, which is shorter than its diff:
```python
import functools

import jax
import jax.numpy as jnp
from jax import lax
from jax.experimental import pallas as pl
from jax.experimental.pallas import tpu as pltpu
from jax.sharding import PartitionSpec as P

REACH_MOST = 8
PIECES = 8
CHUNKS = 4
MESH = pl.DeviceIdType.MESH
F32 = jnp.float32
BF16 = jnp.bfloat16


def iota(shape, dim):
    return lax.broadcasted_iota(jnp.int32, shape, dim)


def kernel(
    n_comp,
    n_tile,
    n_lev,
    state,
    spread,
    fraction,
    blend,
    share,
    weight,
    source,
    used,
    water,
    pond,
    reaction,
    out_state,
    out_water,
    edge,
    edge_in,
    turned,
    gathered,
    mixed,
    emission,
    part,
    part_in,
    near,
    water_in,
    ocean,
    ocean_in,
    edge_send,
    edge_recv,
    lev_send,
    lev_recv,
    comp_send,
    comp_recv,
    part_send,
    part_recv,
    near_send,
    near_recv,
    water_send,
    water_recv,
    ocean_send,
    ocean_recv,
):
    depth, rows, width = state.shape
    levels = blend.shape[1]
    fields = share.shape[0]
    most = weight.shape[1]
    reach = min(REACH_MOST, (n_tile - 1) // 2)
    half = rows // n_comp
    span = rows // CHUNKS
    per_piece = depth // PIECES
    piece_rows = per_piece * rows

    comp = lax.axis_index("comp")
    tile = lax.axis_index("tile")
    lev = lax.axis_index("lev")
    block = comp * n_lev + lev
    half_at = pl.multiple_of(comp * half, half)

    def at(dc=0, dt=0, dl=0):
        return (
            lax.rem(comp + dc, n_comp),
            lax.rem(tile + dt + n_tile, n_tile),
            lax.rem(lev + dl, n_lev),
        )

    group = [(dc, dl) for dc in range(n_comp) for dl in range(n_lev) if dc or dl]
    offsets = [o for d in range(1, reach + 1) for o in (d, -d)]

    def remote(src, dst, send, recv, device):
        copy = pltpu.make_async_remote_copy(
            src_ref=src,
            dst_ref=dst,
            send_sem=send,
            recv_sem=recv,
            device_id=device,
            device_id_type=MESH,
        )
        return copy

    barrier = pltpu.get_barrier_semaphore()
    for dc, dl in group:
        pl.semaphore_signal(barrier, inc=1, device_id=at(dc, 0, dl), device_id_type=MESH)
    for o in offsets:
        pl.semaphore_signal(barrier, inc=1, device_id=at(0, o, 0), device_id_type=MESH)

    row16, col16 = iota((16, width), 0), iota((16, width), 1)
    packed = jnp.zeros((16, piece_rows), F32)
    for p in range(PIECES):
        pick = ((row16 == p) & (col16 == width - 1)) | ((row16 == PIECES + p) & (col16 == 0))
        cells = state[p * per_piece : (p + 1) * per_piece].reshape(piece_rows, width)
        packed += lax.dot_general(
            jnp.where(pick, 1.0, 0.0).astype(BF16),
            cells,
            (((1,), (1,)), ((), ())),
            preferred_element_type=F32,
        )
    edge[...] = packed.astype(BF16)

    own = iota((depth, levels), 1) == iota((depth, levels), 0) + block * depth
    own_share = lax.dot_general(
        jnp.where(own, 1.0, 0.0).astype(BF16),
        share[...],
        (((1,), (1,)), ((), ())),
        preferred_element_type=F32,
    )
    total = jnp.zeros((depth, 1), F32)
    for f in range(fields):
        total += reaction[f] * own_share[:, f : f + 1]
    emission[...] = jnp.broadcast_to(total, (depth, width))

    pl.semaphore_wait(barrier, len(group) + len(offsets))

    edge_copies = []
    for s, o in enumerate((1, -1)):
        copy = remote(edge, edge_in.at[s], edge_send.at[s], edge_recv.at[s], at(0, o, 0))
        copy.start()
        edge_copies.append(copy)
    for copy in edge_copies:
        copy.wait_recv()

    sides = jnp.concatenate([edge_in[0], edge_in[1]], axis=0).astype(F32)
    sides = sides.T.astype(BF16)
    row32, col32 = iota((32, width), 0), iota((32, width), 1)
    lat, lon = iota((rows, width), 0), iota((rows, width), 1)
    rate = spread[...]

    def one_piece(p, emitted):
        place = ((row32 == p) & (col32 == 0)) | (
            (row32 == 16 + PIECES + p) & (col32 == width - 1)
        )
        border = jnp.dot(
            sides, jnp.where(place, 1.0, 0.0).astype(BF16), preferred_element_type=F32
        )
        for q in range(per_piece):
            k = p * per_piece + q
            field = state[k].astype(F32)
            rim = border[q * rows : (q + 1) * rows]
            west = jnp.where(lon == 0, rim, pltpu.roll(field, 1, 1))
            east = jnp.where(lon == width - 1, rim, pltpu.roll(field, width - 1, 1))
            above = jnp.where(lat == rows - 1, 0.0, pltpu.roll(field, rows - 1, 0))
            below = jnp.where(lat == 0, 0.0, pltpu.roll(field, 1, 0))
            lap = above + below + east + west - 4.0 * field
            moved = field + rate * lap - fraction[k] * (field - west)
            moved = moved.astype(BF16).astype(F32)
            turned[pl.ds(k, rows, stride=depth), :] = moved
            emitted = emitted + emission[pl.ds(k, 1), :] * moved
        return emitted

    part[...] = lax.fori_loop(0, PIECES, one_piece, jnp.zeros((rows, width), F32))

    copies = []

    part_copies = []
    for i, (dc, dl) in enumerate(group):
        device = at(dc, 0, dl)
        begin = pl.multiple_of(device[0] * half, half)
        copy = remote(
            part.at[pl.ds(begin, half)], part_in.at[i], part_send.at[i], part_recv.at[i], device
        )
        copy.start()
        part_copies.append(copy)

    lev_copies, comp_copies = {}, {}
    for i in range(CHUNKS):
        lines = turned[i * span * depth : (i + 1) * span * depth]
        gathered[block, i * span : (i + 1) * span] = lines.astype(BF16).reshape(span, depth, width)
        mine = gathered.at[block, pl.ds(i * span, span)]
        for dl in range(1, n_lev):
            copy = remote(
                mine, mine, lev_send.at[dl - 1, i], lev_recv.at[dl - 1, i], at(0, 0, dl)
            )
            copy.start()
            lev_copies[dl, i] = copy
        for dc in range(1, n_comp):
            copy = remote(
                mine, mine, comp_send.at[dc - 1, 0, i], comp_recv.at[dc - 1, 0, i], at(dc, 0, 0)
            )
            copy.start()
            comp_copies[dc, 0, i] = copy

    water_copies = []
    for s, o in enumerate((1, -1)):
        copy = remote(
            water.at[pl.ds(half_at, half)],
            water_in.at[s],
            water_send.at[s],
            water_recv.at[s],
            at(0, o, 0),
        )
        copy.start()
        water_copies.append(copy)

    for copy in part_copies:
        copy.wait_recv()
    flux = part[pl.ds(half_at, half), :]
    for i in range(len(group)):
        flux += part_in[i]
    near[reach] = flux.astype(BF16)
    near_copies = []
    for i, o in enumerate(offsets):
        copy = remote(
            near.at[reach], near.at[reach - o], near_send.at[i], near_recv.at[i], at(0, o, 0)
        )
        copy.start()
        near_copies.append(copy)

    def relay(i):
        for dl in range(1, n_lev):
            lev_copies[dl, i].wait_recv()
            origin = comp * n_lev + lax.rem(lev - dl + n_lev, n_lev)
            theirs = gathered.at[origin, pl.ds(i * span, span)]
            for dc in range(1, n_comp):
                copy = remote(
                    theirs,
                    theirs,
                    comp_send.at[dc - 1, dl, i],
                    comp_recv.at[dc - 1, dl, i],
                    at(dc, 0, 0),
                )
                copy.start()
                comp_copies[dc, dl, i] = copy

    def mix(i):
        for dc in range(1, n_comp):
            for dl in range(n_lev):
                comp_copies[dc, dl, i].wait_recv()
        factor = blend[...]
        for r in range(i * span, (i + 1) * span):
            column = gathered[:, r].reshape(levels, width)
            new = jnp.dot(factor, column, preferred_element_type=F32)
            new += gathered[block, r].astype(F32)
            mixed[pl.ds(r, depth, stride=rows), :] = new
        done = mixed[...].reshape(depth, rows, width)[:, i * span : (i + 1) * span]
        out_state[:, i * span : (i + 1) * span, :] = done.astype(BF16)

    def remap():
        for copy in near_copies:
            copy.wait_recv()
        for copy in water_copies:
            copy.wait_recv()
        picked = []
        for b in range(most):
            slot = lax.rem(source[0, b] - tile + reach + 2 * n_tile, n_tile)
            slot = jnp.minimum(slot, 2 * reach)
            live = jnp.where(b < used[0], 1.0, 0.0).astype(F32)
            picked.append((near[slot].astype(F32) * live).astype(BF16))
        push = jnp.dot(
            jnp.concatenate(picked, axis=1),
            weight[0].reshape(most * width, width),
            preferred_element_type=F32,
        )
        top = water[...]
        above = jnp.where(lat == rows - 1, 0.0, pltpu.roll(top, rows - 1, 0))
        below = jnp.where(lat == 0, 0.0, pltpu.roll(top, 1, 0))
        ocean[...] = above + below - 4.0 * top
        mine = water[pl.ds(half_at, half), :]
        at_lon = iota((half, width), 1)
        west = jnp.where(at_lon == 0, pltpu.roll(water_in[0], 1, 1), pltpu.roll(mine, 1, 1))
        east = jnp.where(
            at_lon == width - 1,
            pltpu.roll(water_in[1], width - 1, 1),
            pltpu.roll(mine, width - 1, 1),
        )
        bend = ocean[pl.ds(half_at, half), :] + west + east
        later = mine + pond[pl.ds(half_at, half), :] * bend + push
        ocean_in[0] = later
        out_water[pl.ds(half_at, half), :] = later
        sent = []
        for dc in range(1, n_comp):
            copy = remote(
                ocean_in.at[0],
                ocean_in.at[dc],
                ocean_send.at[dc - 1],
                ocean_recv.at[dc - 1],
                at(dc, 0, 0),
            )
            copy.start()
            sent.append(copy)
        return sent

    relay(0)
    relay(1)
    mix(0)
    ocean_copies = remap()
    for i in range(2, CHUNKS):
        relay(i)
        mix(i - 1)
    mix(CHUNKS - 1)
    for dc in range(1, n_comp):
        ocean_copies[dc - 1].wait_recv()
        begin = pl.multiple_of(lax.rem(comp - dc + n_comp, n_comp) * half, half)
        out_water[pl.ds(begin, half), :] = ocean_in[dc]

    for copy in edge_copies + part_copies + water_copies + near_copies + ocean_copies:
        copy.wait_send()
    for copy in list(lev_copies.values()) + list(comp_copies.values()):
        copy.wait_send()


def solution(mesh):
    n_comp, n_tile, n_lev = (mesh.shape[a] for a in ("comp", "tile", "lev"))

    def on_device(*args):
        state, spread, fraction, blend, share, weight, source, used, water, pond, reaction = args
        depth, rows, width = state.shape
        reach = min(REACH_MOST, (n_tile - 1) // 2)
        half = rows // n_comp
        peers = n_comp * n_lev - 1
        dma = pltpu.SemaphoreType.DMA
        vmem = pl.BlockSpec(memory_space=pltpu.VMEM)
        smem = pl.BlockSpec(memory_space=pltpu.SMEM)
        piece = depth * rows // PIECES
        return pl.pallas_call(
            functools.partial(kernel, n_comp, n_tile, n_lev),
            out_shape=(
                jax.ShapeDtypeStruct(state.shape, state.dtype),
                jax.ShapeDtypeStruct(water.shape, water.dtype),
            ),
            in_specs=[vmem, vmem, smem, vmem, vmem, vmem, smem, smem, vmem, vmem, smem],
            out_specs=(vmem, vmem),
            scratch_shapes=[
                pltpu.VMEM((16, piece), BF16),
                pltpu.VMEM((2, 16, piece), BF16),
                pltpu.VMEM((rows * depth, width), F32),
                pltpu.VMEM((n_comp * n_lev, rows, depth, width), BF16),
                pltpu.VMEM((depth * rows, width), F32),
                pltpu.VMEM((depth, width), F32),
                pltpu.VMEM((rows, width), F32),
                pltpu.VMEM((peers, half, width), F32),
                pltpu.VMEM((2 * reach + 1, half, width), BF16),
                pltpu.VMEM((2, half, width), F32),
                pltpu.VMEM((rows, width), F32),
                pltpu.VMEM((n_comp, half, width), F32),
                dma((2,)),
                dma((2,)),
                dma((n_lev - 1, CHUNKS)),
                dma((n_lev - 1, CHUNKS)),
                dma((n_comp - 1, n_lev, CHUNKS)),
                dma((n_comp - 1, n_lev, CHUNKS)),
                dma((peers,)),
                dma((peers,)),
                dma((2 * reach,)),
                dma((2 * reach,)),
                dma((2,)),
                dma((2,)),
                dma((n_comp - 1,)),
                dma((n_comp - 1,)),
            ],
            compiler_params=pltpu.CompilerParams(
                collective_id=0, has_side_effects=True, vmem_limit_bytes=32 * 1024 * 1024
            ),
            cost_estimate=pl.CostEstimate(
                flops=200_000_000, bytes_accessed=2_000_000, transcendentals=0
            ),
        )(state, spread, fraction, blend, share, weight, source, used, water, pond, reaction)

    in_specs = (
        P(("comp", "lev"), None, "tile"),
        P(None, "tile"),
        P(("comp", "lev")),
        P(("comp", "lev"), None),
        P(),
        P("tile", None, None, None),
        P("tile", None),
        P("tile"),
        P(None, "tile"),
        P(None, "tile"),
        P(),
    )
    out_specs = (P(("comp", "lev"), None, "tile"), P(None, "tile"))
    return jax.shard_map(
        on_device, mesh=mesh, in_specs=in_specs, out_specs=out_specs, check_vma=False
    )
```

time: 91 us -> 36.1 us (0.40)
  the two profiles are of different devices: /device:TPU:0 before, /device:TPU:1 now
where the time goes in v1:
time: 36.1 us; the launch traced here: 35.6 us
  Pallas kernels  26.4 us (73%)
  local copies, waits for them, and re-layouts  7.77 us (22%)
  between operations  1.35 us (4%)
    pallas_call x1, Pallas kernels, on_device(): pl.pallas_call(functools.partial(kernel, n_comp, n_tile, n_lev), out_shap...  26.4 us
    unnamed x22, local copies, waits for them, and re-layouts  7.77 us

profile of v1, /device:TPU:1, one launch (start us, length us, event | category | flops | bytes accessed | tf_op | source)
XLA Modules:
  0.0 35.6 jit_solution(11698731033258545001)
XLA Ops:
  0.6 0.0 copy-start.6
  0.6 0.0 copy-start.7
  1.3 0.0 copy-done.6
  1.3 0.0 copy-done.7
  1.3 0.0 copy-start
  1.3 1.0 %copy-done = bf16[32,64,128]{2,1,0:T(8,128)(2,1)S(1)} copy-done((bf16[32,64,128]{2,1,0:T(8,128)(2,1)S(1)}, bf16[32,64,128]{2,1,0:T(8,128)(2,1)}, u32[]{:S(2)}) %copy-start) | copy-done | bytes 524312
  2.4 0.0 copy-start.1
  2.4 1.0 %copy-done.1 = bf16[1,16,128,128]{3,2,1,0:T(8,128)(2,1)S(1)} copy-done((bf16[1,16,128,128]{3,2,1,0:T(8,128)(2,1)S(1)}, bf16[1,16,128,128]{3,2,1,0:T(8,128)(2,1)}, u32[]{:S(2)}) %copy-start.1) | copy-done | bytes 524312
  3.4 0.0 copy-start.2
  3.4 0.8 %copy-done.2 = f32[64,128]{1,0:T(8,128)S(1)} copy-done((f32[64,128]{1,0:T(8,128)S(1)}, f32[64,128]{1,0:T(8,128)}, u32[]{:S(2)}) %copy-start.2) | copy-done | bytes 32792
  4.2 0.0 copy-start.3
  4.2 0.8 %copy-done.3 = f32[64,128]{1,0:T(8,128)S(1)} copy-done((f32[64,128]{1,0:T(8,128)S(1)}, f32[64,128]{1,0:T(8,128)}, u32[]{:S(2)}) %copy-start.3) | copy-done | bytes 32792
  4.9 0.0 copy-start.4
  4.9 0.8 %copy-done.4 = f32[64,128]{1,0:T(8,128)S(1)} copy-done((f32[64,128]{1,0:T(8,128)S(1)}, f32[64,128]{1,0:T(8,128)}, u32[]{:S(2)}) %copy-start.4) | copy-done | bytes 32792
  5.7 0.0 copy-start.5
  5.7 0.7 %copy-done.5 = bf16[32,128]{1,0:T(8,128)(2,1)S(1)} copy-done((bf16[32,128]{1,0:T(8,128)(2,1)S(1)}, bf16[32,128]{1,0:T(8,128)(2,1)}, u32[]{:S(2)}) %copy-start.5) | copy-done | bytes 8216
  6.4 0.0 copy-start.8
  6.4 0.7 %copy-done.8 = s32[1,16]{1,0:T(1,128)S(1)} copy-done((s32[1,16]{1,0:T(1,128)S(1)}, s32[1,16]{1,0:T(1,128)}, u32[]{:S(2)}) %copy-start.8) | copy-done | bytes 88
  7.1 0.0 copy-start.9
  7.1 0.7 %copy-done.9 = f32[4]{0:T(128)S(1)} copy-done((f32[4]{0:T(128)S(1)}, f32[4]{0:T(128)}, u32[]{:S(2)}) %copy-start.9) | copy-done | bytes 40
  7.7 26.4 %shard_map.122 = (bf16[32,64,128]{2,1,0:T(8,128)(2,1)S(1)}, f32[64,128]{1,0:T(8,128)S(1)}) custom-call(bf16[32,64,128]{2,1,0:T(8,128)(2,1)S(1)} %copy-done, f32[64,128]{1,0:T(8,128)S(1)} %copy-done.2, f32[32]{0:T(128)S(1)} %copy-done.7, bf16[32,128]{1,0:T(8,128)(2,1)S(1)} %copy-done.5, bf16[4,128]{1,0:T(4,128)(2,1)S(1)} %copy-done.6, ...), custom_call_target="tpu_custom_call" | custom-call | flops 200000000 | bytes 2000000 | tf_op jit(solution)/shard_map/pallas_call | solution.py:336
  34.2 0.8 %copy.16 = bf16[32,64,128]{2,1,0:T(8,128)(2,1)} copy(bf16[32,64,128]{2,1,0:T(8,128)(2,1)S(1)} %get-tuple-element.4) | data formatting | bytes 1048576
  35.0 0.6 %copy.17 = f32[64,128]{1,0:T(8,128)} copy(f32[64,128]{1,0:T(8,128)S(1)} %get-tuple-element.5) | data formatting | bytes 65536
Async XLA Ops:
  0.6 0.7 %copy-start.6 = (bf16[4,128]{1,0:T(4,128)(2,1)S(1)}, bf16[4,128]{1,0:T(4,128)(2,1)}, u32[]{:S(2)}) copy-start(bf16[4,128]{1,0:T(4,128)(2,1)} %share.1) | copy-start | bytes 3076
  0.6 0.7 %copy-start.7 = (f32[32]{0:T(128)S(1)}, f32[32]{0:T(128)}, u32[]{:S(2)}) copy-start(f32[32]{0:T(128)} %fraction.1) | copy-start | bytes 388
  1.3 1.0 %copy-start = (bf16[32,64,128]{2,1,0:T(8,128)(2,1)S(1)}, bf16[32,64,128]{2,1,0:T(8,128)(2,1)}, u32[]{:S(2)}) copy-start(bf16[32,64,128]{2,1,0:T(8,128)(2,1)} %state.1) | copy-start | bytes 1572868
  2.4 1.0 %copy-start.1 = (bf16[1,16,128,128]{3,2,1,0:T(8,128)(2,1)S(1)}, bf16[1,16,128,128]{3,2,1,0:T(8,128)(2,1)}, u32[]{:S(2)}) copy-start(bf16[1,16,128,128]{3,2,1,0:T(8,128)(2,1)} %weight.1) | copy-start | bytes 1572868
  3.4 0.8 %copy-start.2 = (f32[64,128]{1,0:T(8,128)S(1)}, f32[64,128]{1,0:T(8,128)}, u32[]{:S(2)}) copy-start(f32[64,128]{1,0:T(8,128)} %spread.1) | copy-start | bytes 98308
  4.2 0.8 %copy-start.3 = (f32[64,128]{1,0:T(8,128)S(1)}, f32[64,128]{1,0:T(8,128)}, u32[]{:S(2)}) copy-start(f32[64,128]{1,0:T(8,128)} %water.1) | copy-start | bytes 98308
  4.9 0.8 %copy-start.4 = (f32[64,128]{1,0:T(8,128)S(1)}, f32[64,128]{1,0:T(8,128)}, u32[]{:S(2)}) copy-start(f32[64,128]{1,0:T(8,128)} %pond.1) | copy-start | bytes 98308
  5.7 0.7 %copy-start.5 = (bf16[32,128]{1,0:T(8,128)(2,1)S(1)}, bf16[32,128]{1,0:T(8,128)(2,1)}, u32[]{:S(2)}) copy-start(bf16[32,128]{1,0:T(8,128)(2,1)} %blend.1) | copy-start | bytes 24580
  6.4 0.7 %copy-start.8 = (s32[1,16]{1,0:T(1,128)S(1)}, s32[1,16]{1,0:T(1,128)}, u32[]{:S(2)}) copy-start(s32[1,16]{1,0:T(1,128)} %source.1) | copy-start | bytes 196
  7.1 0.7 %copy-start.9 = (f32[4]{0:T(128)S(1)}, f32[4]{0:T(128)}, u32[]{:S(2)}) copy-start(f32[4]{0:T(128)} %reaction.1) | copy-start | bytes 52

commit v2 on v1

--- a/solution.py
+++ b/solution.py
@@ -9,7 +9,8 @@
 
 REACH_MOST = 8
 PIECES = 8
-CHUNKS = 4
+CHUNKS = 8
+EARLY = 4
 MESH = pl.DeviceIdType.MESH
 F32 = jnp.float32
 BF16 = jnp.bfloat16
@@ -23,6 +24,19 @@
     n_comp,
     n_tile,
     n_lev,
+    state_in,
+    spread_in,
+    fraction_in,
+    blend_in,
+    share_in,
+    weight_in,
+    source_in,
+    used_in,
+    water_top_in,
+    pond_in,
+    reaction_in,
+    out_state,
+    out_water,
     state,
     spread,
     fraction,
@@ -34,10 +48,11 @@
     water,
     pond,
     reaction,
-    out_state,
-    out_water,
+    load_sem,
     edge,
     edge_in,
+    patch,
+    patch_turned,
     turned,
     gathered,
     mixed,
@@ -50,6 +65,8 @@
     ocean_in,
     edge_send,
     edge_recv,
+    patch_send,
+    patch_recv,
     lev_send,
     lev_recv,
     comp_send,
@@ -100,25 +117,82 @@
         )
         return copy
 
+    loads = {}
+    for i, (name, src, dst) in enumerate(
+        (
+            ("state", state_in, state),
+            ("share", share_in, share),
+            ("reaction", reaction_in, reaction),
+            ("spread", spread_in, spread),
+            ("fraction", fraction_in, fraction),
+            ("water", water_top_in, water),
+            ("blend", blend_in, blend),
+            ("weight", weight_in, weight),
+            ("source", source_in, source),
+            ("used", used_in, used),
+            ("pond", pond_in, pond),
+        )
+    ):
+        loads[name] = pltpu.make_async_copy(src, dst, load_sem.at[i])
+        loads[name].start()
+
     barrier = pltpu.get_barrier_semaphore()
     for dc, dl in group:
         pl.semaphore_signal(barrier, inc=1, device_id=at(dc, 0, dl), device_id_type=MESH)
     for o in offsets:
         pl.semaphore_signal(barrier, inc=1, device_id=at(0, o, 0), device_id_type=MESH)
 
+    loads["state"].wait()
     row16, col16 = iota((16, width), 0), iota((16, width), 1)
-    packed = jnp.zeros((16, piece_rows), F32)
-    for p in range(PIECES):
-        pick = ((row16 == p) & (col16 == width - 1)) | ((row16 == PIECES + p) & (col16 == 0))
-        cells = state[p * per_piece : (p + 1) * per_piece].reshape(piece_rows, width)
-        packed += lax.dot_general(
-            jnp.where(pick, 1.0, 0.0).astype(BF16),
-            cells,
-            (((1,), (1,)), ((), ())),
-            preferred_element_type=F32,
-        )
-    edge[...] = packed.astype(BF16)
-
+    first, last = col16 == 0, col16 == width - 1
+
+    def pack(cells):
+        packed = jnp.zeros((16, piece_rows), F32)
+        for p in range(PIECES):
+            pick = ((row16 == p) & last) | ((row16 == PIECES + p) & first)
+            packed += lax.dot_general(
+                jnp.where(pick, 1.0, 0.0).astype(BF16),
+                cells(p),
+                (((1,), (1,)), ((), ())),
+                preferred_element_type=F32,
+            )
+        return packed.astype(BF16)
+
+    edge[...] = pack(
+        lambda p: state[p * per_piece : (p + 1) * per_piece].reshape(piece_rows, width)
+    )
+
+    loads["spread"].wait()
+    loads["fraction"].wait()
+    lat, lon = iota((rows, width), 0), iota((rows, width), 1)
+    inside = (lon > 0) & (lon < width - 1)
+    rate = spread[...]
+
+    def step(k, west_edge, east_edge):
+        field = state[k].astype(F32)
+        west, east = pltpu.roll(field, 1, 1), pltpu.roll(field, width - 1, 1)
+        if west_edge is not None:
+            west = jnp.where(lon == 0, west_edge, west)
+            east = jnp.where(lon == width - 1, east_edge, east)
+        above = jnp.where(lat == rows - 1, 0.0, pltpu.roll(field, rows - 1, 0))
+        below = jnp.where(lat == 0, 0.0, pltpu.roll(field, 1, 0))
+        lap = above + below + east + west - 4.0 * field
+        return field + rate * lap - fraction[k] * (field - west)
+
+    def inner_piece(p, carry):
+        for q in range(per_piece):
+            k = p * per_piece + q
+            moved = jnp.where(inside, step(k, None, None), 0.0)
+            turned[pl.ds(k, rows, stride=depth), :] = moved
+        return carry
+
+    lax.fori_loop(0, PIECES, inner_piece, 0)
+    for i in range(CHUNKS):
+        lines = turned[i * span * depth : (i + 1) * span * depth]
+        gathered[block, i * span : (i + 1) * span] = lines.astype(BF16).reshape(span, depth, width)
+
+    loads["share"].wait()
+    loads["reaction"].wait()
     own = iota((depth, levels), 1) == iota((depth, levels), 0) + block * depth
     own_share = lax.dot_general(
         jnp.where(own, 1.0, 0.0).astype(BF16),
@@ -131,6 +205,7 @@
         total += reaction[f] * own_share[:, f : f + 1]
     emission[...] = jnp.broadcast_to(total, (depth, width))
 
+    loads["water"].wait()
     pl.semaphore_wait(barrier, len(group) + len(offsets))
 
     edge_copies = []
@@ -138,55 +213,8 @@
         copy = remote(edge, edge_in.at[s], edge_send.at[s], edge_recv.at[s], at(0, o, 0))
         copy.start()
         edge_copies.append(copy)
-    for copy in edge_copies:
-        copy.wait_recv()
-
-    sides = jnp.concatenate([edge_in[0], edge_in[1]], axis=0).astype(F32)
-    sides = sides.T.astype(BF16)
-    row32, col32 = iota((32, width), 0), iota((32, width), 1)
-    lat, lon = iota((rows, width), 0), iota((rows, width), 1)
-    rate = spread[...]
-
-    def one_piece(p, emitted):
-        place = ((row32 == p) & (col32 == 0)) | (
-            (row32 == 16 + PIECES + p) & (col32 == width - 1)
-        )
-        border = jnp.dot(
-            sides, jnp.where(place, 1.0, 0.0).astype(BF16), preferred_element_type=F32
-        )
-        for q in range(per_piece):
-            k = p * per_piece + q
-            field = state[k].astype(F32)
-            rim = border[q * rows : (q + 1) * rows]
-            west = jnp.where(lon == 0, rim, pltpu.roll(field, 1, 1))
-            east = jnp.where(lon == width - 1, rim, pltpu.roll(field, width - 1, 1))
-            above = jnp.where(lat == rows - 1, 0.0, pltpu.roll(field, rows - 1, 0))
-            below = jnp.where(lat == 0, 0.0, pltpu.roll(field, 1, 0))
-            lap = above + below + east + west - 4.0 * field
-            moved = field + rate * lap - fraction[k] * (field - west)
-            moved = moved.astype(BF16).astype(F32)
-            turned[pl.ds(k, rows, stride=depth), :] = moved
-            emitted = emitted + emission[pl.ds(k, 1), :] * moved
-        return emitted
-
-    part[...] = lax.fori_loop(0, PIECES, one_piece, jnp.zeros((rows, width), F32))
-
-    copies = []
-
-    part_copies = []
-    for i, (dc, dl) in enumerate(group):
-        device = at(dc, 0, dl)
-        begin = pl.multiple_of(device[0] * half, half)
-        copy = remote(
-            part.at[pl.ds(begin, half)], part_in.at[i], part_send.at[i], part_recv.at[i], device
-        )
-        copy.start()
-        part_copies.append(copy)
-
     lev_copies, comp_copies = {}, {}
-    for i in range(CHUNKS):
-        lines = turned[i * span * depth : (i + 1) * span * depth]
-        gathered[block, i * span : (i + 1) * span] = lines.astype(BF16).reshape(span, depth, width)
+    def send_chunk(i):
         mine = gathered.at[block, pl.ds(i * span, span)]
         for dl in range(1, n_lev):
             copy = remote(
@@ -213,6 +241,56 @@
         copy.start()
         water_copies.append(copy)
 
+    for i in range(EARLY):
+        send_chunk(i)
+
+    for copy in edge_copies:
+        copy.wait_recv()
+
+    sides = jnp.concatenate([edge_in[0], edge_in[1]], axis=0).astype(F32)
+    sides = sides.T.astype(BF16)
+    row32, col32 = iota((32, width), 0), iota((32, width), 1)
+
+    def one_piece(p, emitted):
+        place = ((row32 == p) & (col32 == 0)) | (
+            (row32 == 16 + PIECES + p) & (col32 == width - 1)
+        )
+        border = jnp.dot(
+            sides, jnp.where(place, 1.0, 0.0).astype(BF16), preferred_element_type=F32
+        )
+        for q in range(per_piece):
+            k = p * per_piece + q
+            rim = border[q * rows : (q + 1) * rows]
+            moved = step(k, rim, rim).astype(BF16).astype(F32)
+            turned[pl.ds(k, rows, stride=depth), :] = moved
+            emitted = emitted + emission[pl.ds(k, 1), :] * moved
+        return emitted
+
+    part[...] = lax.fori_loop(0, PIECES, one_piece, jnp.zeros((rows, width), F32))
+
+    part_copies = []
+    for i, (dc, dl) in enumerate(group):
+        device = at(dc, 0, dl)
+        begin = pl.multiple_of(device[0] * half, half)
+        copy = remote(
+            part.at[pl.ds(begin, half)], part_in.at[i], part_send.at[i], part_recv.at[i], device
+        )
+        copy.start()
+        part_copies.append(copy)
+
+    patch[block] = pack(
+        lambda p: turned[p * piece_rows : (p + 1) * piece_rows].astype(BF16)
+    )
+    patch_copies = []
+    for i, (dc, dl) in enumerate(group):
+        copy = remote(
+            patch.at[block], patch.at[block], patch_send.at[i], patch_recv.at[i], at(dc, 0, dl)
+        )
+        copy.start()
+        patch_copies.append(copy)
+
+    for i in range(EARLY, CHUNKS):
+        send_chunk(i)
     for copy in part_copies:
         copy.wait_recv()
     flux = part[pl.ds(half_at, half), :]
@@ -248,11 +326,19 @@
             for dl in range(n_lev):
                 comp_copies[dc, dl, i].wait_recv()
         factor = blend[...]
-        for r in range(i * span, (i + 1) * span):
-            column = gathered[:, r].reshape(levels, width)
+        place = ((row16 == i) & last) | ((row16 == PIECES + i) & first)
+        place = jnp.where(place, 1.0, 0.0).astype(BF16)
+        parts = []
+        for b in range(n_comp * n_lev):
+            rim = jnp.dot(patch_turned[b], place, preferred_element_type=F32).astype(BF16)
+            parts.append(gathered[b, i * span : (i + 1) * span].reshape(piece_rows, width) + rim)
+        for r in range(span):
+            lines = slice(r * depth, (r + 1) * depth)
+            column = jnp.concatenate([part[lines] for part in parts], axis=0)
             new = jnp.dot(factor, column, preferred_element_type=F32)
-            new += gathered[block, r].astype(F32)
-            mixed[pl.ds(r, depth, stride=rows), :] = new
+            line = i * span + r
+            new += turned[line * depth : (line + 1) * depth]
+            mixed[pl.ds(line, depth, stride=rows), :] = new
         done = mixed[...].reshape(depth, rows, width)[:, i * span : (i + 1) * span]
         out_state[:, i * span : (i + 1) * span, :] = done.astype(BF16)
 
@@ -301,20 +387,30 @@
             sent.append(copy)
         return sent
 
+    for name in ("blend", "weight", "source", "used", "pond"):
+        loads[name].wait()
     relay(0)
     relay(1)
+    for copy in patch_copies:
+        copy.wait_recv()
+    for b in range(n_comp * n_lev):
+        patch_turned[b] = patch[b].astype(F32).T.astype(BF16)
+    relay(2)
     mix(0)
+    relay(3)
+    mix(1)
     ocean_copies = remap()
-    for i in range(2, CHUNKS):
+    for i in range(4, CHUNKS):
         relay(i)
-        mix(i - 1)
+        mix(i - 2)
+    mix(CHUNKS - 2)
     mix(CHUNKS - 1)
     for dc in range(1, n_comp):
         ocean_copies[dc - 1].wait_recv()
         begin = pl.multiple_of(lax.rem(comp - dc + n_comp, n_comp) * half, half)
         out_water[pl.ds(begin, half), :] = ocean_in[dc]
 
-    for copy in edge_copies + part_copies + water_copies + near_copies + ocean_copies:
+    for copy in edge_copies + patch_copies + part_copies + water_copies + near_copies + ocean_copies:
         copy.wait_send()
     for copy in list(lev_copies.values()) + list(comp_copies.values()):
         copy.wait_send()
@@ -331,7 +427,6 @@
         peers = n_comp * n_lev - 1
         dma = pltpu.SemaphoreType.DMA
         vmem = pl.BlockSpec(memory_space=pltpu.VMEM)
-        smem = pl.BlockSpec(memory_space=pltpu.SMEM)
         piece = depth * rows // PIECES
         return pl.pallas_call(
             functools.partial(kernel, n_comp, n_tile, n_lev),
@@ -339,11 +434,20 @@
                 jax.ShapeDtypeStruct(state.shape, state.dtype),
                 jax.ShapeDtypeStruct(water.shape, water.dtype),
             ),
-            in_specs=[vmem, vmem, smem, vmem, vmem, vmem, smem, smem, vmem, vmem, smem],
+            in_specs=[pl.BlockSpec(memory_space=pltpu.HBM)] * len(args),
             out_specs=(vmem, vmem),
             scratch_shapes=[
+                *(
+                    (pltpu.SMEM if arg.ndim == 1 or arg.dtype == jnp.int32 else pltpu.VMEM)(
+                        arg.shape, arg.dtype
+                    )
+                    for arg in args
+                ),
+                dma((len(args),)),
                 pltpu.VMEM((16, piece), BF16),
                 pltpu.VMEM((2, 16, piece), BF16),
+                pltpu.VMEM((peers + 1, 16, piece), BF16),
+                pltpu.VMEM((peers + 1, piece, 16), BF16),
                 pltpu.VMEM((rows * depth, width), F32),
                 pltpu.VMEM((n_comp * n_lev, rows, depth, width), BF16),
                 pltpu.VMEM((depth * rows, width), F32),
@@ -356,6 +460,8 @@
                 pltpu.VMEM((n_comp, half, width), F32),
                 dma((2,)),
                 dma((2,)),
+                dma((peers,)),
+                dma((peers,)),
                 dma((n_lev - 1, CHUNKS)),
                 dma((n_lev - 1, CHUNKS)),
                 dma((n_comp - 1, n_lev, CHUNKS)),
@@ -370,7 +476,7 @@
                 dma((n_comp - 1,)),
             ],
             compiler_params=pltpu.CompilerParams(
-                collective_id=0, has_side_effects=True, vmem_limit_bytes=32 * 1024 * 1024
+                collective_id=0, has_side_effects=True, vmem_limit_bytes=63 * 1024 * 1024
             ),
             cost_estimate=pl.CostEstimate(
                 flops=200_000_000, bytes_accessed=2_000_000, transcendentals=0

time: 36.1 us -> 28.9 us (0.80)
  the two profiles are of different devices: /device:TPU:1 before, /device:TPU:0 now
where the time goes in v2:
time: 28.9 us; the launch traced here: 28.7 us
  Pallas kernels  24.9 us (86%)
  local copies, waits for them, and re-layouts  2.49 us (9%)
  between operations  1.3 us (4%)
    pallas_call x1, Pallas kernels, on_device(): pl.pallas_call(functools.partial(kernel, n_comp, n_tile, n_lev), out_shap...  24.9 us
    unnamed x4, local copies, waits for them, and re-layouts  2.49 us

profile of v2, /device:TPU:0, one launch (start us, length us, event | category | flops | bytes accessed | tf_op | source)
XLA Modules:
  0.0 28.7 jit_solution(2125824780861004465)
XLA Ops:
  1.3 24.9 %shard_map.122 = (bf16[32,64,128]{2,1,0:T(8,128)(2,1)}, f32[64,128]{1,0:T(8,128)}) custom-call(bf16[32,64,128]{2,1,0:T(8,128)(2,1)} %state_in.1, f32[64,128]{1,0:T(8,128)} %spread_in.1, f32[32]{0:T(128)} %fraction_in.1, bf16[32,128]{1,0:T(8,128)(2,1)} %blend_in.1, bf16[4,128]{1,0:T(4,128)(2,1)} %share_in.1, bf16[1,16,128,128]{3,2,1,0:T(8,128)(2,1)} %weight_in.1, ...), custom_call_target="tpu_custom_call" | custom-call | flops 200000000 | bytes 2000000 | tf_op jit(solution)/shard_map/pallas_call | solution.py:431
  26.2 0.0 copy-start
  26.2 1.9 %copy.16 = bf16[32,64,128]{2,1,0:T(8,128)(2,1)} copy(bf16[32,64,128]{2,1,0:T(8,128)(2,1)} %get-tuple-element.4) | data formatting | bytes 1048576
  28.1 0.0 copy-done
  28.1 0.6 %copy.17 = f32[64,128]{1,0:T(8,128)} copy(f32[64,128]{1,0:T(8,128)S(1)} %copy-done) | data formatting | bytes 65536
Async XLA Ops:
  26.2 1.9 %copy-start = (f32[64,128]{1,0:T(8,128)S(1)}, f32[64,128]{1,0:T(8,128)}, u32[]{:S(2)}) copy-start(f32[64,128]{1,0:T(8,128)} %get-tuple-element.5) | copy-start | bytes 98308

commit v3 on v2

--- a/solution.py
+++ b/solution.py
@@ -399,10 +399,11 @@
     mix(0)
     relay(3)
     mix(1)
-    ocean_copies = remap()
     for i in range(4, CHUNKS):
         relay(i)
         mix(i - 2)
+        if i == 5:
+            ocean_copies = remap()
     mix(CHUNKS - 2)
     mix(CHUNKS - 1)
     for dc in range(1, n_comp):

time: 28.9 us -> 28.5 us (0.986)
  Pallas kernels: 24.9 us -> 24.6 us
    pallas_call x1, Pallas kernels: 24.9 us -> 24.6 us  [on_device(): pl.pallas_call(functools.partial(kernel, n_comp, n_tile, n_lev), out_shap...]
where the time goes in v3:
time: 28.5 us; the launch traced here: 28.3 us
  Pallas kernels  24.6 us (86%)
  local copies, waits for them, and re-layouts  2.49 us (9%)
  between operations  1.3 us (5%)
    pallas_call x1, Pallas kernels, on_device(): pl.pallas_call(functools.partial(kernel, n_comp, n_tile, n_lev), out_shap...  24.6 us
    unnamed x4, local copies, waits for them, and re-layouts  2.49 us

profile of v3, /device:TPU:0, one launch (start us, length us, event | category | flops | bytes accessed | tf_op | source)
XLA Modules:
  0.0 28.3 jit_solution(9057686713440602688)
XLA Ops:
  1.3 24.6 %shard_map.122 = (bf16[32,64,128]{2,1,0:T(8,128)(2,1)}, f32[64,128]{1,0:T(8,128)}) custom-call(bf16[32,64,128]{2,1,0:T(8,128)(2,1)} %state_in.1, f32[64,128]{1,0:T(8,128)} %spread_in.1, f32[32]{0:T(128)} %fraction_in.1, bf16[32,128]{1,0:T(8,128)(2,1)} %blend_in.1, bf16[4,128]{1,0:T(4,128)(2,1)} %share_in.1, bf16[1,16,128,128]{3,2,1,0:T(8,128)(2,1)} %weight_in.1, ...), custom_call_target="tpu_custom_call" | custom-call | flops 200000000 | bytes 2000000 | tf_op jit(solution)/shard_map/pallas_call | solution.py:432
  25.8 0.0 copy-start
  25.9 1.9 %copy.16 = bf16[32,64,128]{2,1,0:T(8,128)(2,1)} copy(bf16[32,64,128]{2,1,0:T(8,128)(2,1)} %get-tuple-element.4) | data formatting | bytes 1048576
  27.7 0.0 copy-done
  27.7 0.6 %copy.17 = f32[64,128]{1,0:T(8,128)} copy(f32[64,128]{1,0:T(8,128)S(1)} %copy-done) | data formatting | bytes 65536
Async XLA Ops:
  25.8 1.9 %copy-start = (f32[64,128]{1,0:T(8,128)S(1)}, f32[64,128]{1,0:T(8,128)}, u32[]{:S(2)}) copy-start(f32[64,128]{1,0:T(8,128)} %get-tuple-element.5) | copy-start | bytes 98308
